TPU v7x, 32 devices: a whole 2x2x4 slice. The times are simulated.
32 devices in a mesh: section: 8 (over z, y), tensor: 4 (over x, core).
Axes of the slice: x: 2, y: 2, z: 4, core: 2. Of those that a mesh axis runs over, the one named last changes fastest.
Arguments:
- inputs: bfloat16 [4, 16, 8192], P(None, 'section', 'tensor'), may hold values from -6 to 6
- cotangent: bfloat16 [4, 16, 8192], P(None, 'section', 'tensor'), may hold values from -1.5 to 1.5
- plan: int32 [4], replicated, may hold values from 0 to 3, each once
- weights: bfloat16 [8, 6656, 8192], P('section', None, 'tensor'), may hold values from -0.0625 to 0.0625
Outputs:
- grads: bfloat16 [8, 6656, 8192], P('section', None, 'tensor')
Inputs may be any that keep to these rules, and one draw needn't show every extreme that they name: `plan`: a permutation of the 4 micro-batches.
All inputs are finite; a program needn't handle non-finite values.
Results may differ from a plain program's by a relative error of at most 0.028.
Values may be sent and summed in bfloat16 or wider, within the bound.
A program may use at most 384 MiB of HBM per device.

v0:
```python
import jax
import jax.numpy as jnp
from jax import lax
from jax.sharding import PartitionSpec as P


def swapped(block, axis, bit):
    count = lax.axis_size(axis)
    route = []
    for low in range(count):
        high = low | 1 << bit
        if high != low and high < count:
            route += [(low, high), (high, low)]
    return lax.ppermute(block, axis, route)


def from_behind(value, axis, steps):
    count = lax.axis_size(axis)
    initial, last = (max(0, -steps), min(count, count - steps))
    return lax.ppermute(value, axis, [(source, source + steps) for source in range(initial, last)])


def silu_slope(pre_sum):
    logistic = jax.nn.sigmoid(pre_sum)
    return logistic * (1.0 + pre_sum * (1.0 - logistic))


def local(inputs, cotangent, plan, weights):
    sections = lax.axis_size("section")
    position = lax.axis_index("section")
    copies = sections // 2
    mirror_bit = copies.bit_length() - 1
    lower_section = position < copies
    all_inputs, all_cots = (
        lax.all_gather(inputs, "section", axis=1, tiled=True),
        lax.all_gather(cotangent, "section", axis=1, tiled=True),
    )
    entering = jnp.take(all_inputs, plan, axis=0)
    own_piece = weights[0]
    batches = entering.shape[0]
    row_count = entering.shape[1]
    piece_rows = own_piece.shape[0]
    columns = own_piece.shape[1]
    blank = jnp.zeros((row_count, piece_rows), jnp.float32)

    def project(values):
        return jnp.einsum("rd,fd->rf", values, own_piece, preferred_element_type=jnp.float32)

    def skip_project(values):
        return blank

    def accumulate(left_rows, right_rows, gradient_sum):
        return gradient_sum + jnp.einsum(
            "rf,rd->fd", left_rows, right_rows, preferred_element_type=jnp.float32
        )

    def skip_accumulate(left_rows, right_rows, gradient_sum):
        return gradient_sum

    gradient_sum = jnp.zeros((piece_rows, columns), jnp.float32)
    received = jnp.zeros((row_count, piece_rows), jnp.bfloat16)
    parked = []
    for moment in range(batches + 2):
        back_micro = moment - 2
        mid_micro = moment - 1
        mid_pick = min(max(mid_micro, 0), batches - 1)
        back_pick = min(max(back_micro, 0), batches - 1)
        pre_sum = blank
        outcome = None
        if moment <= batches:
            fwd_pick = min(moment, batches - 1)
            operand = jnp.where(lower_section, entering[fwd_pick], all_cots[mid_pick])
            active = jnp.where(lower_section, moment < batches, mid_micro >= 0)
            product = lax.cond(active, project, skip_project, operand)
            pre_sum = lax.psum(product.astype(jnp.bfloat16), "tensor").astype(jnp.float32)
            outcome = jnp.where(lower_section, jax.nn.silu(pre_sum), pre_sum).astype(jnp.bfloat16)
        parked_slot = parked[back_micro] if back_micro >= 0 else blank
        sending = jnp.where(lower_section, pre_sum, parked_slot)
        returned = swapped(sending.astype(jnp.bfloat16), "section", mirror_bit).astype(
            sending.dtype
        )
        parked.append(returned)
        if moment >= 1:
            grad_pre = (received.astype(jnp.float32) * silu_slope(returned)).astype(jnp.bfloat16)
            left_rows = jnp.where(lower_section, grad_pre, received)
            right_rows = jnp.where(lower_section, entering[back_pick], all_cots[mid_pick])
            active_back = jnp.where(lower_section, back_micro >= 0, mid_micro < batches)
            gradient_sum = lax.cond(
                active_back, accumulate, skip_accumulate, left_rows, right_rows, gradient_sum
            )
        if moment <= batches:
            from_below = from_behind(outcome, "section", copies)
            from_above = from_behind(outcome, "section", -copies)
            received = jnp.where(lower_section, from_above, from_below)
    return gradient_sum.astype(jnp.bfloat16).reshape(1, piece_rows, columns)


def solution(mesh):
    placed = (
        P(None, "section", "tensor"),
        P(None, "section", "tensor"),
        P(),
        P("section", None, "tensor"),
    )
    return jax.shard_map(
        local, mesh=mesh, in_specs=placed, out_specs=P("section", None, "tensor"), check_vma=False
    )
```

profile of v0, /device:TPU:0, one launch (start us, length us, event | category | flops | bytes accessed | tf_op | source)
XLA Modules:
  0.0 403.9 jit_solution(18141500181956932595)
XLA Ops:
  8.6 32.5 %all_gather.6 = bf16[4,16,2048]{2,0,1:T(4,128)(2,1)S(1)} all-gather(bf16[4,2,2048]{2,0,1:T(4,128)(2,1)S(1)} %copy.9), channel_id=1, replica_groups=mesh['section'=8,'tensor'=4] {'section'}, dimensions={1}, use_global_device_ids=true | all-gather | bytes 294912 | tf_op jit(solution)/shard_map/all_gather | solution.py:35
  42.1 30.7 %all_gather.7 = bf16[4,16,2048]{2,0,1:T(4,128)(2,1)S(1)} all-gather(bf16[4,2,2048]{2,0,1:T(4,128)(2,1)S(1)} %copy.11), channel_id=1, replica_groups=mesh['section'=8,'tensor'=4] {'section'}, dimensions={1}, use_global_device_ids=true | all-gather | bytes 294912 | tf_op jit(solution)/shard_map/all_gather | solution.py:36
  74.0 13.2 %convolution_convert_fusion.2 = bf16[16,6656]{1,0:T(8,128)(2,1)} fusion(pred[]{:T(512)} %lt.7, bf16[4,16,2048]{2,1,0:T(8,128)(2,1)S(1)} %broadcast_select_fusion, bf16[1,16,2048]{2,0,1:T(2,128)(2,1)S(1)} %get-tuple-element.117, bf16[1,6656,2048]{2,1,0:T(8,128)(2,1)} %param.15), kind=kOutput, calls=%fused_computation.12 | convolution fusion | flops 436346880 | bytes 27672576 | tf_op jit(solution)/shard_map/cond/branch_1_fun/rd,fd->rf/dot_general | solution.py:47
  87.2 13.2 %convolution_convert_fusion = bf16[16,6656]{1,0:T(8,128)(2,1)} fusion(pred[]{:T(512)} %lt.7, bf16[4,16,2048]{2,1,0:T(8,128)(2,1)S(1)} %broadcast_select_fusion, bf16[1,16,2048]{2,0,1:T(2,128)(2,1)S(1)} %get-tuple-element.115, bf16[1,6656,2048]{2,1,0:T(8,128)(2,1)} %param.15), kind=kOutput, calls=%fused_computation.10 | convolution fusion | flops 436346880 | bytes 27672576 | tf_op jit(solution)/shard_map/cond/branch_1_fun/rd,fd->rf/dot_general | solution.py:47
  100.4 13.2 %convolution_convert_fusion.1 = bf16[16,6656]{1,0:T(8,128)(2,1)} fusion(pred[]{:T(512)} %lt.7, bf16[4,16,2048]{2,1,0:T(8,128)(2,1)S(1)} %broadcast_select_fusion, bf16[1,16,2048]{2,0,1:T(2,128)(2,1)S(1)} %get-tuple-element.116, bf16[1,6656,2048]{2,1,0:T(8,128)(2,1)} %param.15), kind=kOutput, calls=%fused_computation.11 | convolution fusion | flops 436346880 | bytes 27672576 | tf_op jit(solution)/shard_map/cond/branch_1_fun/rd,fd->rf/dot_general | solution.py:47
  113.9 12.6 %conditional.4 = (bf16[16,6656]{1,0:T(8,128)(2,1)S(1)}) conditional(s32[]{:T(128)} %convert_element_type.132, () %tuple.53, (bf16[16,2048]{1,0:T(8,128)(2,1)S(1)}, bf16[6656,2048]{1,0:T(8,128)(2,1)}) %tuple.86), branch_computations={%region_0.1_spmd, %region_1.2_spmd} | conditional | flops 436207616 | bytes 27541512 | solution.py:74
  113.9 12.6 %fusion.124 = bf16[16,6656]{1,0:T(8,128)(2,1)S(1)} fusion(bf16[16,2048]{1,0:T(8,128)(2,1)S(1)} %get-tuple-element.89, bf16[6656,2048]{1,0:T(8,128)(2,1)} %get-tuple-element.90), kind=kOutput, calls=%fused_computation.165 | convolution fusion | flops 436207616 | bytes 27541504 | tf_op jit(solution)/shard_map/cond/branch_1_fun/rd,fd->rf/dot_general | solution.py:47
  127.1 38.0 %all-reduce.3.cloned.1.call-done = (bf16[16,6656]{1,0:T(8,128)(2,1)}, bf16[16,6656]{1,0:T(8,128)(2,1)}, bf16[16,6656]{1,0:T(8,128)(2,1)}, bf16[16,6656]{1,0:T(8,128)(2,1)}, bf16[16,6656]{1,0:T(8,128)(2,1)}) async-done(((bf16[16,6656]{1,0:T(8,128)(2,1)}, bf16[16,6656]{1,0:T(8,128)(2,1)}, bf16[16,6656]{1,0:T(8,128)(2,1)}, bf16[16,6656]{1,0:T(8,128)(2,1)}, bf16[16,6656]{1,0:T(8,128)(2,1)}), ...) | async-done | bytes 1064976 | tf_op jit(solution)/shard_map/psum | solution.py:75
  171.0 5.5 %collective-permute-start.4 = (bf16[16,6656]{1,0:T(8,128)(2,1)S(1)}, bf16[16,6656]{1,0:T(8,128)(2,1)S(1)}, u32[]{:S(2)}, u32[]{:S(2)}) collective-permute-start(bf16[16,6656]{1,0:T(8,128)(2,1)S(1)} %get-tuple-element.124), channel_id=1, source_target_pairs={{0,16},{4,20},{8,24},{12,28},{1,17},{5,21},{9,25},{13,29},{2,18},{... | collective-permute-start | bytes 638984 | tf_op jit(solution)/shard_map/ppermute | solution.py:20
  177.8 5.5 %collective-permute-start.1 = (bf16[16,6656]{1,0:T(8,128)(2,1)S(1)}, bf16[16,6656]{1,0:T(8,128)(2,1)S(1)}, u32[]{:S(2)}, u32[]{:S(2)}) collective-permute-start(bf16[16,6656]{1,0:T(8,128)(2,1)S(1)} %get-tuple-element.129), channel_id=1, source_target_pairs={{0,16},{4,20},{8,24},{12,28},{1,17},{5,21},{9,25},{13,29},{2,18},{... | collective-permute-start | bytes 638984 | tf_op jit(solution)/shard_map/ppermute | solution.py:20
  183.3 5.5 %collective-permute-done.5 = bf16[16,6656]{1,0:T(8,128)(2,1)S(1)} collective-permute-done((bf16[16,6656]{1,0:T(8,128)(2,1)S(1)}, bf16[16,6656]{1,0:T(8,128)(2,1)S(1)}, u32[]{:S(2)}, u32[]{:S(2)}) %collective-permute-start.5) | collective-permute-done | bytes 213024 | tf_op jit(solution)/shard_map/ppermute | solution.py:14
  190.6 16.5 %collective-permute-done = bf16[16,6656]{1,0:T(8,128)(2,1)S(1)} collective-permute-done((bf16[16,6656]{1,0:T(8,128)(2,1)S(1)}, bf16[16,6656]{1,0:T(8,128)(2,1)S(1)}, u32[]{:S(2)}, u32[]{:S(2)}) %collective-permute-start) | collective-permute-done | bytes 213024 | tf_op jit(solution)/shard_map/ppermute | solution.py:20
  208.4 5.5 %collective-permute-start.8 = (bf16[16,6656]{1,0:T(8,128)(2,1)S(1)}, bf16[16,6656]{1,0:T(8,128)(2,1)S(1)}, u32[]{:S(2)}, u32[]{:S(2)}) collective-permute-start(bf16[16,6656]{1,0:T(8,128)(2,1)S(1)} %get-tuple-element.127), channel_id=1, source_target_pairs={{0,16},{4,20},{8,24},{12,28},{1,17},{5,21},{9,25},{13,29},{2,18},{... | collective-permute-start | bytes 638984 | tf_op jit(solution)/shard_map/ppermute | solution.py:20
  216.5 17.6 %conditional.5 = (f32[6656,2048]{1,0:T(8,128)}) conditional(s32[]{:T(128)} %convert_element_type.133, () %tuple.52, (pred[]{:T(512)}, bf16[16,6656]{1,0:T(8,128)(2,1)S(1)}, bf16[16,6656]{1,0:T(8,128)(2,1)S(1)}, bf16[16,2048]{1,0:T(8,128)(2,1)S(1)}) %tuple.55), branch_computations={%region_4.5_spmd, %region_5.6_spmd} | conditional | flops 436314112 | bytes 55017480 | solution.py:88
  216.5 17.6 %broadcast_in_dim.21 = f32[6656,2048]{1,0:T(8,128)} broadcast(f32[]{:T(128)} %constant.23.clone), dimensions={} | broadcast | bytes 54525956 | tf_op jit(solution)/shard_map/broadcast_in_dim | solution.py:60
  235.4 8.4 %collective-permute-start.11 = (bf16[16,6656]{1,0:T(8,128)(2,1)S(1)}, bf16[16,6656]{1,0:T(8,128)(2,1)S(1)}, u32[]{:S(2)}, u32[]{:S(2)}) collective-permute-start(bf16[16,6656]{1,0:T(8,128)(2,1)S(1)} %get-tuple-element.120), channel_id=1, source_target_pairs={{0,16},{4,20},{8,24},{12,28},{1,17},{5,21},{9,25},{13,29},{2,18},{... | collective-permute-start | bytes 638984 | tf_op jit(solution)/shard_map/ppermute | solution.py:20
  243.9 21.0 %fusion.74 = f32[6656,2048]{1,0:T(8,128)} fusion(bf16[16,6656]{1,0:T(8,128)(2,1)S(1)} %collective-permute-done.6, bf16[16,6656]{1,0:T(8,128)(2,1)S(1)} %collective-permute-done.3, bf16[16,6656]{1,0:T(8,128)(2,1)S(1)} %collective-permute-done.4, pred[]{:T(512)} %lt.7, bf16[4,16,2048]{2,1,0:T(8,128)(2,1)S(1)} %broadcast_select_fusion, ...), kind=kOutput, calls=%fused_computation.110 | convolution fusion | flops 437624832 | bytes 55362560 | tf_op jit(solution)/shard_map/cond/branch_1_fun/rf,rd->fd/dot_general | solution.py:53
  266.4 5.7 %collective-permute-start.14 = (bf16[16,6656]{1,0:T(8,128)(2,1)S(1)}, bf16[16,6656]{1,0:T(8,128)(2,1)S(1)}, u32[]{:S(2)}, u32[]{:S(2)}) collective-permute-start(bf16[16,6656]{1,0:T(8,128)(2,1)S(1)} %get-tuple-element.118), channel_id=1, source_target_pairs={{0,16},{4,20},{8,24},{12,28},{1,17},{5,21},{9,25},{13,29},{2,18},{... | collective-permute-start | bytes 638984 | tf_op jit(solution)/shard_map/ppermute | solution.py:20
  272.3 21.0 %fusion.76 = f32[6656,2048]{1,0:T(8,128)} fusion(bf16[16,6656]{1,0:T(8,128)(2,1)S(1)} %collective-permute-done.9, bf16[16,6656]{1,0:T(8,128)(2,1)S(1)} %collective-permute-done.7, bf16[16,6656]{1,0:T(8,128)(2,1)S(1)} %collective-permute-done.8, pred[]{:T(512)} %lt.7, bf16[4,16,2048]{2,1,0:T(8,128)(2,1)S(1)} %broadcast_select_fusion, ...), kind=kOutput, calls=%fused_computation.111 | convolution fusion | flops 437624832 | bytes 55362560 | tf_op jit(solution)/shard_map/cond/branch_1_fun/rf,rd->fd/dot_general | solution.py:53
  293.2 2.9 collective-permute-start.12
  296.4 3.6 collective-permute-done.12
  300.0 68.9 %add_add_fusion = f32[6656,2048]{1,0:T(8,128)} fusion(f32[6656,2048]{1,0:T(8,128)} %fusion.76, f32[6656,2048]{1,0:T(8,128)} %get-tuple-element.138, f32[6656,2048]{1,0:T(8,128)} %fusion.74, bf16[16,6656]{1,0:T(8,128)(2,1)S(1)} %collective-permute-done.12, bf16[16,6656]{1,0:T(8,128)(2,1)S(1)} %collective-permute-done.10, ...), kind=kOutput, calls=%fused_computation.9 | convolution fusion | flops 478519296 | bytes 218940416 | tf_op jit(solution)/shard_map/cond/branch_1_fun/rf,rd->fd/dot_general | solution.py:53
  368.9 28.1 %conditional.7 = (bf16[1,6656,2048]{2,1,0:T(8,128)(2,1)}) conditional(s32[]{:T(128)} %convert_element_type.132, f32[6656,2048]{1,0:T(8,128)} %add_add_fusion, (pred[]{:T(512)}, bf16[16,6656]{1,0:T(8,128)(2,1)S(1)}, bf16[16,6656]{1,0:T(8,128)(2,1)S(1)}, bf16[16,2048]{1,0:T(8,128)(2,1)S(1)}, f32[6656,2048]{1,0:T(8,128)}) %tuple.87), branch_computations={%region_11.12_spmd, %region_12.13_spmd} | conditional | flops 463577088 | bytes 82280456 | solution.py:88
  368.9 28.1 %fusion.3 = bf16[1,6656,2048]{2,1,0:T(8,128)(2,1)} fusion(f32[6656,2048]{1,0:T(8,128)} %get-tuple-element.97, bf16[16,2048]{1,0:T(8,128)(2,1)S(1)} %get-tuple-element.101, bf16[16,6656]{1,0:T(8,128)(2,1)S(1)} %get-tuple-element.99, bf16[16,6656]{1,0:T(8,128)(2,1)S(1)} %get-tuple-element.100, pred[]{:T(512)} %get-tuple-element.98), kind=kOutput, calls=%fused_computation.6 | convolution fusion | flops 463577088 | bytes 82280448 | tf_op jit(solution)/shard_map/cond/branch_1_fun/rf,rd->fd/dot_general | solution.py:53
  (54 shorter events, 21.1 us)
Async XLA Ops:
  6.5 158.6 %all-reduce.3.cloned.1.call-start = ((), (), s32[]{:S(2)}) async-start(), calls=%async_computation | async-start | bytes 2129920 | tf_op jit(solution)/shard_map/psum | solution.py:75
  74.0 39.6 %copy-start.2 = (bf16[16,2048]{1,0:T(8,128)(2,1)}, bf16[16,2048]{1,0:T(8,128)(2,1)S(1)}, u32[]{:S(2)}) copy-start(bf16[16,2048]{1,0:T(8,128)(2,1)S(1)} %get-tuple-element.112) | copy-start | bytes 196612
  113.9 12.6 %copy-start = (bf16[16,6656]{1,0:T(8,128)(2,1)}, bf16[16,6656]{1,0:T(8,128)(2,1)S(1)}, u32[]{:S(2)}) copy-start(bf16[16,6656]{1,0:T(8,128)(2,1)S(1)} %get-tuple-element.139) | copy-start | bytes 638980
  126.4 0.7 copy-start.1
  166.2 22.6 %collective-permute-start.5 = (bf16[16,6656]{1,0:T(8,128)(2,1)S(1)}, bf16[16,6656]{1,0:T(8,128)(2,1)S(1)}, u32[]{:S(2)}, u32[]{:S(2)}) collective-permute-start(bf16[16,6656]{1,0:T(8,128)(2,1)S(1)} %get-tuple-element.128), channel_id=1, source_target_pairs={{0,16},{16,0},{4,20},{20,4},{8,24},{24,8},{12,28},{28,12},{1,17},{... | collective-permute-start | bytes 638984 | tf_op jit(solution)/shard_map/ppermute | solution.py:14
  169.7 64.4 %collective-permute-start.3 = (bf16[16,6656]{1,0:T(8,128)(2,1)S(1)}, bf16[16,6656]{1,0:T(8,128)(2,1)S(1)}, u32[]{:S(2)}, u32[]{:S(2)}) collective-permute-start(bf16[16,6656]{1,0:T(8,128)(2,1)S(1)} %get-tuple-element.124), channel_id=1, source_target_pairs={{16,0},{20,4},{24,8},{28,12},{17,1},{21,5},{25,9},{29,13},{18,2},{... | collective-permute-start | bytes 638984 | tf_op jit(solution)/shard_map/ppermute | solution.py:20
  171.0 64.4 %collective-permute-start.4 = (bf16[16,6656]{1,0:T(8,128)(2,1)S(1)}, bf16[16,6656]{1,0:T(8,128)(2,1)S(1)}, u32[]{:S(2)}, u32[]{:S(2)}) collective-permute-start(bf16[16,6656]{1,0:T(8,128)(2,1)S(1)} %get-tuple-element.124), channel_id=1, source_target_pairs={{0,16},{4,20},{8,24},{12,28},{1,17},{5,21},{9,25},{13,29},{2,18},{... | collective-permute-start | bytes 638984 | tf_op jit(solution)/shard_map/ppermute | solution.py:20
  176.5 30.6 %collective-permute-start = (bf16[16,6656]{1,0:T(8,128)(2,1)S(1)}, bf16[16,6656]{1,0:T(8,128)(2,1)S(1)}, u32[]{:S(2)}, u32[]{:S(2)}) collective-permute-start(bf16[16,6656]{1,0:T(8,128)(2,1)S(1)} %get-tuple-element.129), channel_id=1, source_target_pairs={{16,0},{20,4},{24,8},{28,12},{17,1},{21,5},{25,9},{29,13},{18,2},{... | collective-permute-start | bytes 638984 | tf_op jit(solution)/shard_map/ppermute | solution.py:20
  177.8 30.6 %collective-permute-start.1 = (bf16[16,6656]{1,0:T(8,128)(2,1)S(1)}, bf16[16,6656]{1,0:T(8,128)(2,1)S(1)}, u32[]{:S(2)}, u32[]{:S(2)}) collective-permute-start(bf16[16,6656]{1,0:T(8,128)(2,1)S(1)} %get-tuple-element.129), channel_id=1, source_target_pairs={{0,16},{4,20},{8,24},{12,28},{1,17},{5,21},{9,25},{13,29},{2,18},{... | collective-permute-start | bytes 638984 | tf_op jit(solution)/shard_map/ppermute | solution.py:20
  188.8 26.4 %collective-permute-start.2 = (bf16[16,6656]{1,0:T(8,128)(2,1)S(1)}, bf16[16,6656]{1,0:T(8,128)(2,1)S(1)}, u32[]{:S(2)}, u32[]{:S(2)}) collective-permute-start(bf16[16,6656]{1,0:T(8,128)(2,1)S(1)} %get-tuple-element.125), channel_id=1, source_target_pairs={{0,16},{16,0},{4,20},{20,4},{8,24},{24,8},{12,28},{28,12},{1,17},{... | collective-permute-start | bytes 638984 | tf_op jit(solution)/shard_map/ppermute | solution.py:14
  207.1 59.4 %collective-permute-start.7 = (bf16[16,6656]{1,0:T(8,128)(2,1)S(1)}, bf16[16,6656]{1,0:T(8,128)(2,1)S(1)}, u32[]{:S(2)}, u32[]{:S(2)}) collective-permute-start(bf16[16,6656]{1,0:T(8,128)(2,1)S(1)} %get-tuple-element.127), channel_id=1, source_target_pairs={{16,0},{20,4},{24,8},{28,12},{17,1},{21,5},{25,9},{29,13},{18,2},{... | collective-permute-start | bytes 638984 | tf_op jit(solution)/shard_map/ppermute | solution.py:20
  208.4 63.8 %collective-permute-start.8 = (bf16[16,6656]{1,0:T(8,128)(2,1)S(1)}, bf16[16,6656]{1,0:T(8,128)(2,1)S(1)}, u32[]{:S(2)}, u32[]{:S(2)}) collective-permute-start(bf16[16,6656]{1,0:T(8,128)(2,1)S(1)} %get-tuple-element.127), channel_id=1, source_target_pairs={{0,16},{4,20},{8,24},{12,28},{1,17},{5,21},{9,25},{13,29},{2,18},{... | collective-permute-start | bytes 638984 | tf_op jit(solution)/shard_map/ppermute | solution.py:20
  215.2 28.6 %collective-permute-start.6 = (bf16[16,6656]{1,0:T(8,128)(2,1)}, bf16[16,6656]{1,0:T(8,128)(2,1)S(1)}, u32[]{:S(2)}, u32[]{:S(2)}) collective-permute-start(bf16[16,6656]{1,0:T(8,128)(2,1)} %get-tuple-element.126), channel_id=1, source_target_pairs={{0,16},{16,0},{4,20},{20,4},{8,24},{24,8},{12,28},{28,12},{1,17},{... | collective-permute-start | bytes 638984 | tf_op jit(solution)/shard_map/ppermute | solution.py:14
  234.1 62.3 %collective-permute-start.10 = (bf16[16,6656]{1,0:T(8,128)(2,1)S(1)}, bf16[16,6656]{1,0:T(8,128)(2,1)S(1)}, u32[]{:S(2)}, u32[]{:S(2)}) collective-permute-start(bf16[16,6656]{1,0:T(8,128)(2,1)S(1)} %get-tuple-element.120), channel_id=1, source_target_pairs={{16,0},{20,4},{24,8},{28,12},{17,1},{21,5},{25,9},{29,13},{18,2},{... | collective-permute-start | bytes 638984 | tf_op jit(solution)/shard_map/ppermute | solution.py:20
  235.4 61.0 %collective-permute-start.11 = (bf16[16,6656]{1,0:T(8,128)(2,1)S(1)}, bf16[16,6656]{1,0:T(8,128)(2,1)S(1)}, u32[]{:S(2)}, u32[]{:S(2)}) collective-permute-start(bf16[16,6656]{1,0:T(8,128)(2,1)S(1)} %get-tuple-element.120), channel_id=1, source_target_pairs={{0,16},{4,20},{8,24},{12,28},{1,17},{5,21},{9,25},{13,29},{2,18},{... | collective-permute-start | bytes 638984 | tf_op jit(solution)/shard_map/ppermute | solution.py:20
  243.8 21.1 %copy-start.4 = (bf16[16,6656]{1,0:T(8,128)(2,1)S(1)}, bf16[16,6656]{1,0:T(8,128)(2,1)}, u32[]{:S(2)}) copy-start(bf16[16,6656]{1,0:T(8,128)(2,1)} %get-tuple-element.107) | copy-start | bytes 638980
  243.9 21.2 %collective-permute-start.9 = (bf16[16,6656]{1,0:T(8,128)(2,1)S(1)}, bf16[16,6656]{1,0:T(8,128)(2,1)S(1)}, u32[]{:S(2)}, u32[]{:S(2)}) collective-permute-start(bf16[16,6656]{1,0:T(8,128)(2,1)S(1)} %get-tuple-element.121), channel_id=1, source_target_pairs={{0,16},{16,0},{4,20},{20,4},{8,24},{24,8},{12,28},{28,12},{1,17},{... | collective-permute-start | bytes 638984 | tf_op jit(solution)/shard_map/ppermute | solution.py:14
  265.1 28.2 %collective-permute-start.13 = (bf16[16,6656]{1,0:T(8,128)(2,1)S(1)}, bf16[16,6656]{1,0:T(8,128)(2,1)S(1)}, u32[]{:S(2)}, u32[]{:S(2)}) collective-permute-start(bf16[16,6656]{1,0:T(8,128)(2,1)S(1)} %get-tuple-element.118), channel_id=1, source_target_pairs={{16,0},{20,4},{24,8},{28,12},{17,1},{21,5},{25,9},{29,13},{18,2},{... | collective-permute-start | bytes 638984 | tf_op jit(solution)/shard_map/ppermute | solution.py:20
  266.4 29.7 %collective-permute-start.14 = (bf16[16,6656]{1,0:T(8,128)(2,1)S(1)}, bf16[16,6656]{1,0:T(8,128)(2,1)S(1)}, u32[]{:S(2)}, u32[]{:S(2)}) collective-permute-start(bf16[16,6656]{1,0:T(8,128)(2,1)S(1)} %get-tuple-element.118), channel_id=1, source_target_pairs={{0,16},{4,20},{8,24},{12,28},{1,17},{5,21},{9,25},{13,29},{2,18},{... | collective-permute-start | bytes 638984 | tf_op jit(solution)/shard_map/ppermute | solution.py:20
  272.2 24.0 %collective-permute-start.15 = (bf16[16,6656]{1,0:T(8,128)(2,1)S(1)}, bf16[16,6656]{1,0:T(8,128)(2,1)S(1)}, u32[]{:S(2)}, u32[]{:S(2)}) collective-permute-start(bf16[16,6656]{1,0:T(8,128)(2,1)S(1)} %fusion.41), channel_id=1, source_target_pairs={{0,16},{16,0},{4,20},{20,4},{8,24},{24,8},{12,28},{28,12},{1,17},{... | collective-permute-start | bytes 638984 | tf_op jit(solution)/shard_map/ppermute | solution.py:14
  293.2 6.7 %collective-permute-start.12 = (bf16[16,6656]{1,0:T(8,128)(2,1)S(1)}, bf16[16,6656]{1,0:T(8,128)(2,1)S(1)}, u32[]{:S(2)}, u32[]{:S(2)}) collective-permute-start(bf16[16,6656]{1,0:T(8,128)(2,1)S(1)} %get-tuple-element.119), channel_id=1, source_target_pairs={{0,16},{16,0},{4,20},{20,4},{8,24},{24,8},{12,28},{28,12},{1,17},{... | collective-permute-start | bytes 638984 | tf_op jit(solution)/shard_map/ppermute | solution.py:14
  296.4 72.6 %copy-start.3 = (bf16[16,2048]{1,0:T(8,128)(2,1)S(1)}, bf16[16,2048]{1,0:T(8,128)(2,1)}, u32[]{:S(2)}) copy-start(bf16[16,2048]{1,0:T(8,128)(2,1)} %copy-done.2) | copy-start | bytes 196612
Sparse Core Ops, SparseCore 0:
  127.3 37.8 all-reduce.2
where the time goes:
time: 404 us
  matrix products  191 us (47%)
  waiting for transfers between devices  65 us (16%)
  blocking collectives  63.3 us (16%)
  starting transfers between devices  42.5 us (11%)
  local copies, waits for them, and re-layouts  20.9 us (5%)
  between operations  13.7 us (3%)
  other arithmetic  7.05 us (2%)
    dot_general x4, matrix products, accumulate(): jnp.einsum('rf,rd->fd', left_rows, right_rows, preferred_element_type=jnp...  139 us
    dot_general x4, matrix products, project(): jnp.einsum('rd,fd->rf', values, own_piece, preferred_element_type=jnp.flo...  52.2 us
    psum x1, waiting for transfers between devices, local(): lax.psum(product.astype(jnp.bfloat16), 'tensor').astype(jnp.float32)  38 us
    ppermute x10, starting transfers between devices, from_behind(): lax.ppermute(value, axis, [(source, source + steps) for source in range(i...  37 us
    all_gather x1, blocking collectives, local(): lax.all_gather(inputs, 'section', axis=1, tiled=True)  32.5 us
    all_gather x1, blocking collectives, local(): lax.all_gather(cotangent, 'section', axis=1, tiled=True)  30.7 us
    broadcast_in_dim x1, local copies, waits for them, and re-layouts, local(): gradient_sum = jnp.zeros((piece_rows, columns), jnp.float32)  17.6 us
    ppermute x10, waiting for transfers between devices, from_behind(): lax.ppermute(value, axis, [(source, source + steps) for source in range(i...  16.5 us
  transfers between devices with their start and end apart: 17, of which 5 were waited for; matrix products, arithmetic and copies ran while one was open for 16% of the time, Pallas kernels for 0%

commit v1 on v0

v1 whole, which is shorter than its diff:
```python
import functools

import jax
import jax.numpy as jnp
from jax import lax
from jax.experimental import pallas as pl
from jax.experimental.pallas import tpu as pltpu
from jax.sharding import PartitionSpec as P

MESH = pl.DeviceIdType.MESH
CHUNKS = 4


def unit_of(hidden):
    return hidden // 13 if hidden % (13 * 128) == 0 else 128


def chunk_bounds(hidden):
    unit = unit_of(hidden)
    units = hidden // unit
    count = min(CHUNKS, units)
    edges = [-(-units * c // count) for c in range(count + 1)]
    return [(low * unit, (high - low) * unit) for low, high in zip(edges, edges[1:])]


def exchange_kernel(
    sections, tensors, bounds, unit,
    mine_ref, weight_hbm, left_ref, right_ref,
    weight, gathered, part, partial_in, kept, swap_out, swap_in,
    weight_sem, gather_send, gather_recv, reduce_send, reduce_recv,
    swap_send, swap_recv, spread_send, spread_recv,
):
    position = lax.axis_index("section")
    rank = lax.axis_index("tensor")
    half = sections // 2
    lower = position < half
    mirror = lax.rem(position + half, sections)
    row_count = right_ref.shape[0]
    block_rows = row_count // tensors

    loads = []
    for c, (low, size) in enumerate(bounds):
        rows = pl.ds(low, size)
        load = pltpu.make_async_copy(weight_hbm.at[rows], weight.at[rows], weight_sem.at[c])
        load.start()
        loads.append(load)

    barrier = pltpu.get_barrier_semaphore()
    for step in range(1, sections):
        other = lax.rem(position + step, sections)
        pl.semaphore_signal(barrier, inc=1, device_id=(other, rank), device_id_type=MESH)
    for step in range(1, tensors):
        other = lax.rem(rank + step, tensors)
        pl.semaphore_signal(barrier, inc=1, device_id=(position, other), device_id_type=MESH)
    pl.semaphore_wait(barrier, sections + tensors - 2)

    gathers = []
    for step in range(1, sections):
        other = lax.rem(position + step, sections)
        copy = pltpu.make_async_remote_copy(
            src_ref=mine_ref.at[other // half],
            dst_ref=gathered.at[position],
            send_sem=gather_send.at[step],
            recv_sem=gather_recv.at[step],
            device_id=(other, rank),
            device_id_type=MESH,
        )
        copy.start()
        gathers.append(copy)
    gathered[position] = mine_ref[position // half]
    for copy in gathers:
        copy.wait_recv()
    shard_rows = gathered.shape[1] // 2
    for pair in range(sections // 2):
        stacked = []
        for source in (2 * pair, 2 * pair + 1):
            block = gathered[source].astype(jnp.float32)
            stacked.append(jnp.concatenate([block[:shard_rows], block[shard_rows:]], axis=1))
        rows = pl.ds(2 * pair * shard_rows, 2 * shard_rows)
        right_ref[rows, :] = jnp.concatenate(stacked, axis=0).astype(jnp.bfloat16)

    def project(c):
        low, size = bounds[c]
        loads[c].wait()

        def tile(index, carry):
            start = pl.multiple_of(low + index * unit, 128)
            product = lax.dot_general(
                right_ref[...], weight[pl.ds(start, unit), :],
                (((1,), (1,)), ((), ())), preferred_element_type=jnp.float32,
            ).astype(jnp.bfloat16)
            for t in range(tensors):
                part[t, :, pl.ds(start, unit)] = product[t * block_rows:(t + 1) * block_rows]
            return carry

        lax.fori_loop(0, size // unit, tile, 0)
        lanes = pl.ds(low, size)
        copies = []
        for step in range(1, tensors):
            other = lax.rem(rank + step, tensors)
            copy = pltpu.make_async_remote_copy(
                src_ref=part.at[other, :, lanes],
                dst_ref=partial_in.at[step, :, lanes],
                send_sem=reduce_send.at[c, step],
                recv_sem=reduce_recv.at[c, step],
                device_id=(position, other),
                device_id_type=MESH,
            )
            copy.start()
            copies.append(copy)
        return copies

    def reduce(c, copies):
        low, size = bounds[c]
        lanes = pl.ds(low, size)
        for copy in copies:
            copy.wait_recv()
        pre_sum = part[rank, :, lanes].astype(jnp.float32)
        for step in range(1, tensors):
            pre_sum = pre_sum + partial_in[step, :, lanes].astype(jnp.float32)
        kept[:, lanes] = pre_sum
        hidden = pre_sum * jax.nn.sigmoid(pre_sum)
        swap_out[:, lanes] = jnp.where(lower, hidden, pre_sum).astype(jnp.bfloat16)
        copy = pltpu.make_async_remote_copy(
            src_ref=swap_out.at[:, lanes],
            dst_ref=swap_in.at[:, lanes],
            send_sem=swap_send.at[c],
            recv_sem=swap_recv.at[c],
            device_id=(mirror, rank),
            device_id_type=MESH,
        )
        copy.start()
        return copy

    def finish(c, swap):
        low, size = bounds[c]
        lanes = pl.ds(low, size)
        swap.wait_recv()
        pre_sum = kept[:, lanes]
        logistic = jax.nn.sigmoid(pre_sum)
        slope = logistic * (1.0 + pre_sum * (1.0 - logistic))
        received = swap_in[:, lanes].astype(jnp.float32)
        left_ref[rank, :, lanes] = jnp.where(lower, received * slope, received).astype(jnp.bfloat16)
        copies = []
        for step in range(1, tensors):
            other = lax.rem(rank + step, tensors)
            copy = pltpu.make_async_remote_copy(
                src_ref=left_ref.at[rank, :, lanes],
                dst_ref=left_ref.at[rank, :, lanes],
                send_sem=spread_send.at[c, step],
                recv_sem=spread_recv.at[c, step],
                device_id=(position, other),
                device_id_type=MESH,
            )
            copy.start()
            copies.append(copy)
        return copies

    count = len(bounds)
    reductions, swaps, spreads = [], [], []
    for moment in range(count + 2):
        if moment < count:
            reductions.append(project(moment))
        if 0 <= moment - 1 < count:
            swaps.append(reduce(moment - 1, reductions[moment - 1]))
        if 0 <= moment - 2 < count:
            spreads.append(finish(moment - 2, swaps[moment - 2]))
    for copies in spreads:
        for copy in copies:
            copy.wait_recv()
    for copy in gathers + sum(reductions, []) + swaps + sum(spreads, []):
        copy.wait_send()


def gradient_kernel(left_ref, right_ref, out_ref):
    rows = right_ref.shape[0]
    left = left_ref[...].reshape(rows, left_ref.shape[2])
    out_ref[...] = lax.dot_general(
        left, right_ref[...], (((0,), (0,)), ((), ())), preferred_element_type=jnp.float32
    ).astype(out_ref.dtype)


def local(sections, tensors, inputs, cotangent, plan, weights):
    batches, tokens, columns = inputs.shape
    hidden = weights.shape[1]
    shard_rows = batches * tokens
    row_count = shard_rows * sections
    block_rows = row_count // tensors
    unit = unit_of(hidden)
    bounds = chunk_bounds(hidden)
    count = len(bounds)

    entering = []
    for k in range(batches):
        row = inputs[0]
        for micro in range(1, batches):
            row = jnp.where(plan[k] == micro, inputs[micro], row)
        entering.append(row)
    mine = jnp.stack([jnp.stack(entering), cotangent])
    mine = mine.reshape(2, shard_rows, 2, columns // 2).transpose(0, 2, 1, 3)
    mine = mine.reshape(2, 2 * shard_rows, columns // 2)

    dma = pltpu.SemaphoreType.DMA
    left, right = pl.pallas_call(
        functools.partial(exchange_kernel, sections, tensors, bounds, unit),
        out_shape=(
            jax.ShapeDtypeStruct((tensors, block_rows, hidden), jnp.bfloat16),
            jax.ShapeDtypeStruct((row_count, columns), jnp.bfloat16),
        ),
        in_specs=[pl.BlockSpec(memory_space=pltpu.VMEM), pl.BlockSpec(memory_space=pl.ANY)],
        out_specs=(pl.BlockSpec(memory_space=pltpu.VMEM), pl.BlockSpec(memory_space=pltpu.VMEM)),
        scratch_shapes=[
            pltpu.VMEM((hidden, columns), jnp.bfloat16),
            pltpu.VMEM((sections, 2 * shard_rows, columns // 2), jnp.bfloat16),
            pltpu.VMEM((tensors, block_rows, hidden), jnp.bfloat16),
            pltpu.VMEM((tensors, block_rows, hidden), jnp.bfloat16),
            pltpu.VMEM((block_rows, hidden), jnp.float32),
            pltpu.VMEM((block_rows, hidden), jnp.bfloat16),
            pltpu.VMEM((block_rows, hidden), jnp.bfloat16),
            dma((count,)),
            dma((sections,)),
            dma((sections,)),
            dma((count, tensors)),
            dma((count, tensors)),
            dma((count,)),
            dma((count,)),
            dma((count, tensors)),
            dma((count, tensors)),
        ],
        compiler_params=pltpu.CompilerParams(
            collective_id=0, has_side_effects=True, vmem_limit_bytes=56 * 1024 * 1024
        ),
        cost_estimate=pl.CostEstimate(
            flops=2 * row_count * hidden * columns,
            bytes_accessed=2 * hidden * columns,
            transcendentals=2 * block_rows * hidden,
        ),
    )(mine, weights[0])

    grads = pl.pallas_call(
        gradient_kernel,
        grid=(hidden // unit,),
        out_shape=jax.ShapeDtypeStruct((hidden, columns), jnp.bfloat16),
        in_specs=[
            pl.BlockSpec((tensors, block_rows, unit), lambda i: (0, 0, i)),
            pl.BlockSpec((row_count, columns), lambda i: (0, 0)),
        ],
        out_specs=pl.BlockSpec((unit, columns), lambda i: (i, 0)),
        compiler_params=pltpu.CompilerParams(vmem_limit_bytes=40 * 1024 * 1024),
        cost_estimate=pl.CostEstimate(
            flops=2 * row_count * hidden * columns,
            bytes_accessed=2 * hidden * columns,
            transcendentals=0,
        ),
    )(left, right)
    return grads.reshape(1, hidden, columns)


def solution(mesh):
    placed = (
        P(None, "section", "tensor"),
        P(None, "section", "tensor"),
        P(),
        P("section", None, "tensor"),
    )
    return jax.shard_map(
        functools.partial(local, mesh.shape["section"], mesh.shape["tensor"]),
        mesh=mesh, in_specs=placed, out_specs=P("section", None, "tensor"), check_vma=False,
    )
```

time: 404 us -> 70.3 us (0.17)
  the two profiles are of different devices: /device:TPU:0 before, /device:TPU:13 now
where the time goes in v1:
time: 70.3 us; the launch traced here: 69.8 us
  Pallas kernels  55.3 us (79%)
  between operations  7.82 us (11%)
  local copies, waits for them, and re-layouts  4.39 us (6%)
  other arithmetic  2.25 us (3%)
    pallas_call x1, Pallas kernels, local(): pl.pallas_call(functools.partial(exchange_kernel, sections, tensors, boun...  40.9 us
    pallas_call x1, Pallas kernels, local(): pl.pallas_call(gradient_kernel, grid=(hidden // unit,), out_shape=jax.Sha...  14.4 us
    unnamed x4, local copies, waits for them, and re-layouts  2.1 us
    select_n x2, other arithmetic, local(): row = jnp.where(plan[k] == micro, inputs[micro], row)  1.56 us
    slice x1, local copies, waits for them, and re-layouts, local(): row = jnp.where(plan[k] == micro, inputs[micro], row)  1.46 us

profile of v1, /device:TPU:13, one launch (start us, length us, event | category | flops | bytes accessed | tf_op | source)
XLA Modules:
  0.0 69.8 jit_solution(12611983218595879056)
XLA Ops:
  0.0 1.5 %fusion = (s32[1]{0:T(128)}, s32[1]{0:T(128)}, s32[1]{0:T(128)}, s32[1]{0:T(128)}) fusion(s32[4]{0:T(128)} %param.6), kind=kLoop, calls=%fused_computation.14 | loop fusion | bytes 32 | tf_op jit(solution)/shard_map/slice | solution.py:197
  9.2 0.8 %broadcast_select_fusion.11 = (bf16[1,2,2048]{2,1,0:T(2,128)(2,1)S(1)}, bf16[1,2,2048]{2,1,0:T(2,128)(2,1)S(1)}) fusion(pred[]{:T(512)} %bitcast, pred[]{:T(512)} %bitcast.1, pred[]{:T(512)} %bitcast.2, bf16[4,2,2048]{2,1,0:T(2,128)(2,1)} %param.4, pred[]{:T(512)} %bitcast.8, pred[]{:T(512)} %bitcast.7, pred[]{:T(512)} %bitcast.6), kind=kLoop, calls=%fused_computation.13 | loop fusion | flops 24576 | bytes 49158 | tf_op jit(solution)/shard_map/jit(_where)/select_n | solution.py:197
  10.0 0.8 %broadcast_select_fusion.8 = (bf16[1,2,2048]{2,1,0:T(2,128)(2,1)S(1)}, bf16[1,2,2048]{2,1,0:T(2,128)(2,1)S(1)}) fusion(pred[]{:T(512)} %bitcast.3, pred[]{:T(512)} %bitcast.4, pred[]{:T(512)} %bitcast.5, bf16[4,2,2048]{2,1,0:T(2,128)(2,1)} %param.4, pred[]{:T(512)} %bitcast.11, pred[]{:T(512)} %bitcast.10, pred[]{:T(512)} %bitcast.9), kind=kLoop, calls=%fused_computation.10 | loop fusion | flops 24576 | bytes 49158 | tf_op jit(solution)/shard_map/jit(_where)/select_n | solution.py:197
  10.8 0.1 pad_maximum_fusion
  10.9 0.8 %stack.18 = bf16[1,8,2,1024]{3,2,1,0:T(2,128)(2,1)S(1)} reshape(bf16[4,2,2048]{2,1,0:T(2,128)(2,1)} %param.5) | data formatting | bytes 65536 | tf_op jit(solution)/shard_map/stack | solution.py:199
  11.7 0.6 maximum_bitcast_fusion.mine_ref
  12.3 40.9 %shard_map.46 = (bf16[4,16,6656]{2,1,0:T(8,128)(2,1)}, bf16[64,2048]{1,0:T(8,128)(2,1)}) custom-call(bf16[2,16,1024]{2,1,0:T(8,128)(2,1)} %maximum_bitcast_fusion.mine_ref, bf16[6656,2048]{1,0:T(8,128)(2,1)} %bitcast.18), custom_call_target="tpu_custom_call" | custom-call | flops 1744830464 | bytes 27262976 | tf_op jit(solution)/shard_map/pallas_call | solution.py:204
  53.3 0.0 copy-start
  53.3 1.1 %copy-done = bf16[4,16,6656]{2,1,0:T(8,128)(2,1)S(1)} copy-done((bf16[4,16,6656]{2,1,0:T(8,128)(2,1)S(1)}, bf16[4,16,6656]{2,1,0:T(8,128)(2,1)}, u32[]{:S(2)}) %copy-start) | copy-done | bytes 851992
  54.4 0.0 copy-start.1
  54.5 0.9 %copy-done.1 = bf16[64,2048]{1,0:T(8,128)(2,1)S(1)} copy-done((bf16[64,2048]{1,0:T(8,128)(2,1)S(1)}, bf16[64,2048]{1,0:T(8,128)(2,1)}, u32[]{:S(2)}) %copy-start.1) | copy-done | bytes 262168
  55.4 14.4 %shard_map.47 = bf16[6656,2048]{1,0:T(8,128)(2,1)} custom-call(bf16[4,16,6656]{2,1,0:T(8,128)(2,1)S(1)} %copy-done, bf16[64,2048]{1,0:T(8,128)(2,1)S(1)} %copy-done.1), custom_call_target="tpu_custom_call" | custom-call | flops 1744830464 | bytes 27262976 | tf_op jit(solution)/shard_map/pallas_call | solution.py:240
  (3 shorter events, 0.0 us)
Async XLA Ops:
  53.3 1.2 %copy-start = (bf16[4,16,6656]{2,1,0:T(8,128)(2,1)S(1)}, bf16[4,16,6656]{2,1,0:T(8,128)(2,1)}, u32[]{:S(2)}) copy-start(bf16[4,16,6656]{2,1,0:T(8,128)(2,1)} %get-tuple-element.7.left_ref) | copy-start | bytes 2555908
  54.4 0.9 %copy-start.1 = (bf16[64,2048]{1,0:T(8,128)(2,1)S(1)}, bf16[64,2048]{1,0:T(8,128)(2,1)}, u32[]{:S(2)}) copy-start(bf16[64,2048]{1,0:T(8,128)(2,1)} %get-tuple-element.8.right_ref) | copy-start | bytes 786436

commit v2 on v1

v2 whole, which is shorter than its diff:
```python
import functools

import jax
import jax.numpy as jnp
from jax import lax
from jax.experimental import pallas as pl
from jax.experimental.pallas import tpu as pltpu
from jax.sharding import PartitionSpec as P

MESH = pl.DeviceIdType.MESH
CHUNKS = 5


def unit_of(hidden):
    return hidden // 13 if hidden % (13 * 128) == 0 else 128


def chunk_bounds(hidden):
    unit = unit_of(hidden)
    units = hidden // unit
    count = min(CHUNKS, units)
    edges = [-(-units * c // count) for c in range(count + 1)]
    return [(low * unit, (high - low) * unit) for low, high in zip(edges, edges[1:])]


def exchange_kernel(
    sections, tensors, bounds, unit,
    plan_ref, inputs_ref, cotangent_ref, weight_hbm, left_ref, right_ref,
    weight, stage, mine, gathered, part, pair_in, pair_sum, far_in, kept, swap_out, swap_in,
    weight_sem, gather_send, gather_recv, near_send, near_recv, far_send, far_recv,
    swap_send, swap_recv, wide_send, wide_recv, close_send, close_recv,
):
    position = lax.axis_index("section")
    rank = lax.axis_index("tensor")
    half = sections // 2
    lower = position < half
    mirror = lax.rem(position + half, sections)
    groups = tensors // 2
    parity = lax.rem(rank, 2)
    group = rank // 2
    buddy = rank + 1 - 2 * parity
    row_count = right_ref.shape[0]
    block_rows = row_count // tensors
    batches, tokens, columns = inputs_ref.shape

    barrier = pltpu.get_barrier_semaphore()
    for step in range(1, sections):
        other = lax.rem(position + step, sections)
        pl.semaphore_signal(barrier, inc=1, device_id=(other, rank), device_id_type=MESH)
    for step in range(1, groups):
        other = 2 * lax.rem(group + step, groups) + parity
        pl.semaphore_signal(barrier, inc=1, device_id=(position, other), device_id_type=MESH)
    pl.semaphore_signal(barrier, inc=1, device_id=(position, buddy), device_id_type=MESH)

    loads = []
    for c, (low, size) in enumerate(bounds):
        rows = pl.ds(low, size)
        load = pltpu.make_async_copy(weight_hbm.at[rows], weight.at[rows], weight_sem.at[c])
        load.start()
        loads.append(load)

    for k in range(batches):
        rows = pl.ds(k * tokens, tokens)
        stage[0, rows, :] = inputs_ref[plan_ref[k]].astype(jnp.float32)
        stage[1, rows, :] = cotangent_ref[k].astype(jnp.float32)
    for side in range(2):
        block = stage[side]
        mine[side] = jnp.concatenate(
            [block[:, :columns // 2], block[:, columns // 2:]], axis=0
        ).astype(jnp.bfloat16)

    pl.semaphore_wait(barrier, sections - 1 + groups)

    gathers = []
    for step in range(1, sections):
        other = lax.rem(position + step, sections)
        copy = pltpu.make_async_remote_copy(
            src_ref=mine.at[other // half],
            dst_ref=gathered.at[position],
            send_sem=gather_send.at[step],
            recv_sem=gather_recv.at[step],
            device_id=(other, rank),
            device_id_type=MESH,
        )
        copy.start()
        gathers.append(copy)
    gathered[position] = mine[position // half]
    for copy in gathers:
        copy.wait_recv()
    shard_rows = batches * tokens
    for pair in range(sections // 2):
        stacked = []
        for source in (2 * pair, 2 * pair + 1):
            block = gathered[source].astype(jnp.float32)
            stacked.append(jnp.concatenate([block[:shard_rows], block[shard_rows:]], axis=1))
        rows = pl.ds(2 * pair * shard_rows, 2 * shard_rows)
        right_ref[rows, :] = jnp.concatenate(stacked, axis=0).astype(jnp.bfloat16)

    def project(c):
        low, size = bounds[c]
        loads[c].wait()

        def tile(index, carry):
            start = pl.multiple_of(low + index * unit, 128)
            product = lax.dot_general(
                right_ref[...], weight[pl.ds(start, unit), :],
                (((1,), (1,)), ((), ())), preferred_element_type=jnp.float32,
            ).astype(jnp.bfloat16)
            for t in range(tensors):
                part[t % 2, t // 2, :, pl.ds(start, unit)] = product[t * block_rows:(t + 1) * block_rows]
            return carry

        lax.fori_loop(0, size // unit, tile, 0)
        lanes = pl.ds(low, size)
        copy = pltpu.make_async_remote_copy(
            src_ref=part.at[1 - parity, :, :, lanes],
            dst_ref=pair_in.at[:, :, lanes],
            send_sem=near_send.at[c],
            recv_sem=near_recv.at[c],
            device_id=(position, buddy),
            device_id_type=MESH,
        )
        copy.start()
        return copy

    def pair_up(c, near):
        low, size = bounds[c]
        lanes = pl.ds(low, size)
        near.wait_recv()
        copies = []
        for step in range(1, groups):
            other = lax.rem(group + step, groups)
            pair_sum[step, :, lanes] = (
                part[parity, other, :, lanes].astype(jnp.float32)
                + pair_in[other, :, lanes].astype(jnp.float32)
            ).astype(jnp.bfloat16)
            copy = pltpu.make_async_remote_copy(
                src_ref=pair_sum.at[step, :, lanes],
                dst_ref=far_in.at[step, :, lanes],
                send_sem=far_send.at[c, step],
                recv_sem=far_recv.at[c, step],
                device_id=(position, 2 * other + parity),
                device_id_type=MESH,
            )
            copy.start()
            copies.append(copy)
        return copies

    def reduce(c, far):
        low, size = bounds[c]
        lanes = pl.ds(low, size)
        pre_sum = part[parity, group, :, lanes].astype(jnp.float32)
        pre_sum = pre_sum + pair_in[group, :, lanes].astype(jnp.float32)
        for copy in far:
            copy.wait_recv()
        for step in range(1, groups):
            pre_sum = pre_sum + far_in[step, :, lanes].astype(jnp.float32)
        logistic = jax.nn.sigmoid(pre_sum)
        kept[:, lanes] = logistic * (1.0 + pre_sum * (1.0 - logistic))
        swap_out[:, lanes] = jnp.where(lower, pre_sum * logistic, pre_sum).astype(jnp.bfloat16)
        copy = pltpu.make_async_remote_copy(
            src_ref=swap_out.at[:, lanes],
            dst_ref=swap_in.at[:, lanes],
            send_sem=swap_send.at[c],
            recv_sem=swap_recv.at[c],
            device_id=(mirror, rank),
            device_id_type=MESH,
        )
        copy.start()
        return copy

    def hand_over(c, step):
        low, size = bounds[c]
        source = 2 * lax.rem(group - step + groups, groups) + parity
        block = left_ref.at[source, :, pl.ds(low, size)]
        copy = pltpu.make_async_remote_copy(
            src_ref=block,
            dst_ref=block,
            send_sem=close_send.at[c, step],
            recv_sem=close_recv.at[c, step],
            device_id=(position, buddy),
            device_id_type=MESH,
        )
        copy.start()
        return copy

    def finish(c, swap):
        low, size = bounds[c]
        lanes = pl.ds(low, size)
        swap.wait_recv()
        received = swap_in[:, lanes].astype(jnp.float32)
        left_ref[rank, :, lanes] = jnp.where(
            lower, received * kept[:, lanes], received
        ).astype(jnp.bfloat16)
        copies = []
        for step in range(1, groups):
            other = 2 * lax.rem(group + step, groups) + parity
            copy = pltpu.make_async_remote_copy(
                src_ref=left_ref.at[rank, :, lanes],
                dst_ref=left_ref.at[rank, :, lanes],
                send_sem=wide_send.at[c, step],
                recv_sem=wide_recv.at[c, step],
                device_id=(position, other),
                device_id_type=MESH,
            )
            copy.start()
            copies.append(copy)
        return copies, hand_over(c, 0)

    def forward(c, wide):
        copies = []
        for step in range(1, groups):
            wide[step - 1].wait_recv()
            copies.append(hand_over(c, step))
        return copies

    count = len(bounds)
    nears, fars, swaps, wides, closes = [], [], [], [], []
    for moment in range(count + 4):
        if moment < count:
            nears.append(project(moment))
        if 0 <= moment - 1 < count:
            fars.append(pair_up(moment - 1, nears[moment - 1]))
        if 0 <= moment - 2 < count:
            swaps.append(reduce(moment - 2, fars[moment - 2]))
        if 0 <= moment - 3 < count:
            wide, close = finish(moment - 3, swaps[moment - 3])
            wides.append(wide)
            closes.append(close)
        if 0 <= moment - 4 < count:
            closes.extend(forward(moment - 4, wides[moment - 4]))
    for copy in closes:
        copy.wait_recv()
    for copy in gathers + nears + sum(fars, []) + swaps + sum(wides, []) + closes:
        copy.wait_send()


SLOTS = 4


def gradient_kernel(height, left_ref, right_ref, out_hbm, tiles, sems):
    rows, columns = right_ref.shape
    count = out_hbm.shape[0] // height
    width = min(256, columns)

    def copy_out(index, slot):
        start = pl.multiple_of(index * height, height)
        return pltpu.make_async_copy(tiles.at[slot], out_hbm.at[pl.ds(start, height)], sems.at[slot])

    def tile(index, carry):
        slot = lax.rem(index, SLOTS)

        @pl.when(index >= SLOTS)
        def _():
            copy_out(index - SLOTS, slot).wait()

        start = pl.multiple_of(index * height, height)
        left = left_ref[:, :, pl.ds(start, height)].reshape(rows, height)
        for low in range(0, columns, width):
            tiles[slot, :, low:low + width] = lax.dot_general(
                left, right_ref[:, low:low + width],
                (((0,), (0,)), ((), ())), preferred_element_type=jnp.float32,
            ).astype(tiles.dtype)
        copy_out(index, slot).start()
        return carry

    lax.fori_loop(0, count, tile, 0)
    for index in range(max(0, count - SLOTS), count):
        copy_out(index, index % SLOTS).wait()


def local(sections, tensors, inputs, cotangent, plan, weights):
    batches, tokens, columns = inputs.shape
    hidden = weights.shape[1]
    shard_rows = batches * tokens
    row_count = shard_rows * sections
    block_rows = row_count // tensors
    groups = tensors // 2
    unit = unit_of(hidden)
    bounds = chunk_bounds(hidden)
    count = len(bounds)
    vmem = pl.BlockSpec(memory_space=pltpu.VMEM)

    dma = pltpu.SemaphoreType.DMA
    left, right = pl.pallas_call(
        functools.partial(exchange_kernel, sections, tensors, bounds, unit),
        out_shape=(
            jax.ShapeDtypeStruct((tensors, block_rows, hidden), jnp.bfloat16),
            jax.ShapeDtypeStruct((row_count, columns), jnp.bfloat16),
        ),
        in_specs=[pl.BlockSpec(memory_space=pltpu.SMEM), vmem, vmem, pl.BlockSpec(memory_space=pl.ANY)],
        out_specs=(vmem, vmem),
        scratch_shapes=[
            pltpu.VMEM((hidden, columns), jnp.bfloat16),
            pltpu.VMEM((2, shard_rows, columns), jnp.float32),
            pltpu.VMEM((2, 2 * shard_rows, columns // 2), jnp.bfloat16),
            pltpu.VMEM((sections, 2 * shard_rows, columns // 2), jnp.bfloat16),
            pltpu.VMEM((2, groups, block_rows, hidden), jnp.bfloat16),
            pltpu.VMEM((groups, block_rows, hidden), jnp.bfloat16),
            pltpu.VMEM((groups, block_rows, hidden), jnp.bfloat16),
            pltpu.VMEM((groups, block_rows, hidden), jnp.bfloat16),
            pltpu.VMEM((block_rows, hidden), jnp.float32),
            pltpu.VMEM((block_rows, hidden), jnp.bfloat16),
            pltpu.VMEM((block_rows, hidden), jnp.bfloat16),
            dma((count,)),
            dma((sections,)),
            dma((sections,)),
            dma((count,)),
            dma((count,)),
            dma((count, groups)),
            dma((count, groups)),
            dma((count,)),
            dma((count,)),
            dma((count, groups)),
            dma((count, groups)),
            dma((count, groups)),
            dma((count, groups)),
        ],
        compiler_params=pltpu.CompilerParams(
            collective_id=0, has_side_effects=True, vmem_limit_bytes=56 * 1024 * 1024
        ),
        cost_estimate=pl.CostEstimate(
            flops=2 * row_count * hidden * columns,
            bytes_accessed=2 * hidden * columns,
            transcendentals=2 * block_rows * hidden,
        ),
    )(plan, inputs, cotangent, weights[0])

    height = next(h for h in (256, 128) if hidden % h == 0)
    grads = pl.pallas_call(
        functools.partial(gradient_kernel, height),
        out_shape=jax.ShapeDtypeStruct((hidden, columns), jnp.bfloat16),
        in_specs=[vmem, vmem],
        out_specs=pl.BlockSpec(memory_space=pl.ANY),
        scratch_shapes=[pltpu.VMEM((SLOTS, height, columns), jnp.bfloat16), dma((SLOTS,))],
        compiler_params=pltpu.CompilerParams(vmem_limit_bytes=60 * 1024 * 1024),
        cost_estimate=pl.CostEstimate(
            flops=2 * row_count * hidden * columns,
            bytes_accessed=2 * hidden * columns,
            transcendentals=0,
        ),
    )(left, right)
    return grads.reshape(1, hidden, columns)


def solution(mesh):
    placed = (
        P(None, "section", "tensor"),
        P(None, "section", "tensor"),
        P(),
        P("section", None, "tensor"),
    )
    return jax.shard_map(
        functools.partial(local, mesh.shape["section"], mesh.shape["tensor"]),
        mesh=mesh, in_specs=placed, out_specs=P("section", None, "tensor"), check_vma=False,
    )
```

time: 70.3 us -> 53.8 us (0.77)
  the two profiles are of different devices: /device:TPU:13 before, /device:TPU:0 now
where the time goes in v2:
time: 53.8 us; the launch traced here: 53.5 us
  Pallas kernels  53.5 us (99%)
    pallas_call x1, Pallas kernels, local(): pl.pallas_call(functools.partial(exchange_kernel, sections, tensors, boun...  39.3 us
    pallas_call x1, Pallas kernels, local(): pl.pallas_call(functools.partial(gradient_kernel, height), out_shape=jax....  14.1 us

profile of v2, /device:TPU:0, one launch (start us, length us, event | category | flops | bytes accessed | tf_op | source)
XLA Modules:
  0.0 53.5 jit_solution(7335696539899728829)
XLA Ops:
  0.0 39.3 %shard_map.46 = (bf16[4,16,6656]{2,1,0:T(8,128)(2,1)}, bf16[64,2048]{1,0:T(8,128)(2,1)}) custom-call(s32[4]{0:T(128)} %plan_ref.1, bf16[4,2,2048]{2,1,0:T(2,128)(2,1)} %inputs_ref.1, bf16[4,2,2048]{2,1,0:T(2,128)(2,1)} %cotangent_ref.1, bf16[6656,2048]{1,0:T(8,128)(2,1)} %bitcast.2), custom_call_target="tpu_custom_call" | custom-call | flops 1744830464 | bytes 27262976 | tf_op jit(solution)/shard_map/pallas_call | solution.py:285
  39.4 14.1 %shard_map.47 = bf16[6656,2048]{1,0:T(8,128)(2,1)} custom-call(bf16[4,16,6656]{2,1,0:T(8,128)(2,1)} %get-tuple-element.7.left_ref, bf16[64,2048]{1,0:T(8,128)(2,1)} %get-tuple-element.8.right_ref), custom_call_target="tpu_custom_call" | custom-call | flops 1744830464 | bytes 27262976 | tf_op jit(solution)/shard_map/pallas_call | solution.py:330

commit v3 on v2

--- a/solution.py
+++ b/solution.py
@@ -103,9 +103,9 @@
         def tile(index, carry):
             start = pl.multiple_of(low + index * unit, 128)
             product = lax.dot_general(
-                right_ref[...], weight[pl.ds(start, unit), :],
+                weight[pl.ds(start, unit), :], right_ref[...],
                 (((1,), (1,)), ((), ())), preferred_element_type=jnp.float32,
-            ).astype(jnp.bfloat16)
+            ).T.astype(jnp.bfloat16)
             for t in range(tensors):
                 part[t % 2, t // 2, :, pl.ds(start, unit)] = product[t * block_rows:(t + 1) * block_rows]
             return carry
@@ -233,40 +233,6 @@
         copy.wait_recv()
     for copy in gathers + nears + sum(fars, []) + swaps + sum(wides, []) + closes:
         copy.wait_send()
-
-
-SLOTS = 4
-
-
-def gradient_kernel(height, left_ref, right_ref, out_hbm, tiles, sems):
-    rows, columns = right_ref.shape
-    count = out_hbm.shape[0] // height
-    width = min(256, columns)
-
-    def copy_out(index, slot):
-        start = pl.multiple_of(index * height, height)
-        return pltpu.make_async_copy(tiles.at[slot], out_hbm.at[pl.ds(start, height)], sems.at[slot])
-
-    def tile(index, carry):
-        slot = lax.rem(index, SLOTS)
-
-        @pl.when(index >= SLOTS)
-        def _():
-            copy_out(index - SLOTS, slot).wait()
-
-        start = pl.multiple_of(index * height, height)
-        left = left_ref[:, :, pl.ds(start, height)].reshape(rows, height)
-        for low in range(0, columns, width):
-            tiles[slot, :, low:low + width] = lax.dot_general(
-                left, right_ref[:, low:low + width],
-                (((0,), (0,)), ((), ())), preferred_element_type=jnp.float32,
-            ).astype(tiles.dtype)
-        copy_out(index, slot).start()
-        return carry
-
-    lax.fori_loop(0, count, tile, 0)
-    for index in range(max(0, count - SLOTS), count):
-        copy_out(index, index % SLOTS).wait()
 
 
 def local(sections, tensors, inputs, cotangent, plan, weights):
@@ -326,20 +292,10 @@
         ),
     )(plan, inputs, cotangent, weights[0])
 
-    height = next(h for h in (256, 128) if hidden % h == 0)
-    grads = pl.pallas_call(
-        functools.partial(gradient_kernel, height),
-        out_shape=jax.ShapeDtypeStruct((hidden, columns), jnp.bfloat16),
-        in_specs=[vmem, vmem],
-        out_specs=pl.BlockSpec(memory_space=pl.ANY),
-        scratch_shapes=[pltpu.VMEM((SLOTS, height, columns), jnp.bfloat16), dma((SLOTS,))],
-        compiler_params=pltpu.CompilerParams(vmem_limit_bytes=60 * 1024 * 1024),
-        cost_estimate=pl.CostEstimate(
-            flops=2 * row_count * hidden * columns,
-            bytes_accessed=2 * hidden * columns,
-            transcendentals=0,
-        ),
-    )(left, right)
+    grads = lax.dot_general(
+        left.reshape(row_count, hidden), right, (((0,), (0,)), ((), ())),
+        preferred_element_type=jnp.float32,
+    ).astype(jnp.bfloat16)
     return grads.reshape(1, hidden, columns)
 
 

time: 53.8 us -> 54.1 us (level)
  matrix products: 0 us -> 14.4 us
  Pallas kernels: 53.5 us -> 39.2 us
    dot_general x0 -> x1, matrix products: none -> 14.4 us  [local(): lax.dot_general(left.reshape(row_count, hidden), right, (((0,), (0,)), ((...]
    pallas_call x1 -> x0, Pallas kernels: 14.1 us -> none  [local(): pl.pallas_call(functools.partial(gradient_kernel, height), out_shape=jax....]
where the time goes in v3:
time: 54.1 us; the launch traced here: 53.7 us
  Pallas kernels  39.2 us (72%)
  matrix products  14.4 us (27%)
    pallas_call x1, Pallas kernels, local(): pl.pallas_call(functools.partial(exchange_kernel, sections, tensors, boun...  39.2 us
    dot_general x1, matrix products, local(): lax.dot_general(left.reshape(row_count, hidden), right, (((0,), (0,)), ((...  14.4 us

profile of v3, /device:TPU:0, one launch (start us, length us, event | category | flops | bytes accessed | tf_op | source)
XLA Modules:
  0.0 53.7 jit_solution(14059069209347670336)
XLA Ops:
  0.0 39.2 %shard_map.46 = (bf16[4,16,6656]{2,1,0:T(8,128)(2,1)}, bf16[64,2048]{1,0:T(8,128)(2,1)}) custom-call(s32[4]{0:T(128)} %plan_ref.1, bf16[4,2,2048]{2,1,0:T(2,128)(2,1)} %inputs_ref.1, bf16[4,2,2048]{2,1,0:T(2,128)(2,1)} %cotangent_ref.1, bf16[6656,2048]{1,0:T(8,128)(2,1)} %bitcast.6), custom_call_target="tpu_custom_call" | custom-call | flops 1744830464 | bytes 27262976 | tf_op jit(solution)/shard_map/pallas_call | solution.py:251
  39.3 14.4 %convert_bitcast_fusion = bf16[1,6656,2048]{2,1,0:T(8,128)(2,1)} fusion(bf16[64,6656]{1,0:T(8,128)(2,1)} %bitcast.7, bf16[64,2048]{1,0:T(8,128)(2,1)} %get-tuple-element.8), kind=kOutput, calls=%fused_computation | convolution fusion | flops 1758461952 | bytes 28377088 | tf_op jit(solution)/shard_map/dot_general | solution.py:295

commit v4 on v2

--- a/solution.py
+++ b/solution.py
@@ -8,7 +8,8 @@
 from jax.sharding import PartitionSpec as P
 
 MESH = pl.DeviceIdType.MESH
-CHUNKS = 5
+CHUNKS = 7
+EARLY = 3
 
 
 def unit_of(hidden):
@@ -25,10 +26,10 @@
 
 def exchange_kernel(
     sections, tensors, bounds, unit,
-    plan_ref, inputs_ref, cotangent_ref, weight_hbm, left_ref, right_ref,
-    weight, stage, mine, gathered, part, pair_in, pair_sum, far_in, kept, swap_out, swap_in,
+    plan_ref, inputs_ref, cotangent_ref, weight_hbm, left_ref, right_ref, early_hbm,
+    weight, stage, mine, gathered, part, pair_in, pair_sum, far_in, kept, swap_out, swap_in, tiles,
     weight_sem, gather_send, gather_recv, near_send, near_recv, far_send, far_recv,
-    swap_send, swap_recv, wide_send, wide_recv, close_send, close_recv,
+    swap_send, swap_recv, wide_send, wide_recv, close_send, close_recv, early_sem,
 ):
     position = lax.axis_index("section")
     rank = lax.axis_index("tensor")
@@ -52,12 +53,12 @@
         pl.semaphore_signal(barrier, inc=1, device_id=(position, other), device_id_type=MESH)
     pl.semaphore_signal(barrier, inc=1, device_id=(position, buddy), device_id_type=MESH)
 
-    loads = []
-    for c, (low, size) in enumerate(bounds):
-        rows = pl.ds(low, size)
-        load = pltpu.make_async_copy(weight_hbm.at[rows], weight.at[rows], weight_sem.at[c])
-        load.start()
-        loads.append(load)
+    def load(index):
+        rows = pl.ds(pl.multiple_of(index * unit, 128), unit)
+        return pltpu.make_async_copy(weight_hbm.at[rows], weight.at[rows], weight_sem.at[index])
+
+    for index in range(weight.shape[0] // unit):
+        load(index).start()
 
     for k in range(batches):
         rows = pl.ds(k * tokens, tokens)
@@ -98,14 +99,14 @@
 
     def project(c):
         low, size = bounds[c]
-        loads[c].wait()
 
         def tile(index, carry):
+            load(low // unit + index).wait()
             start = pl.multiple_of(low + index * unit, 128)
             product = lax.dot_general(
-                right_ref[...], weight[pl.ds(start, unit), :],
+                weight[pl.ds(start, unit), :], right_ref[...],
                 (((1,), (1,)), ((), ())), preferred_element_type=jnp.float32,
-            ).astype(jnp.bfloat16)
+            ).T.astype(jnp.bfloat16)
             for t in range(tensors):
                 part[t % 2, t // 2, :, pl.ds(start, unit)] = product[t * block_rows:(t + 1) * block_rows]
             return carry
@@ -214,8 +215,20 @@
             copies.append(hand_over(c, step))
         return copies
 
+    def early_tile(index):
+        def store(low, width, value):
+            tiles[index, :, low:low + width] = value
+
+        outer_tile(left_ref, right_ref, index * unit, unit, store)
+        copy = pltpu.make_async_copy(
+            tiles.at[index], early_hbm.at[pl.ds(index * unit, unit)], early_sem.at[index]
+        )
+        copy.start()
+        return copy
+
     count = len(bounds)
-    nears, fars, swaps, wides, closes = [], [], [], [], []
+    arrived = 0
+    nears, fars, swaps, wides, closes, earlies = [], [], [], [], [], []
     for moment in range(count + 4):
         if moment < count:
             nears.append(project(moment))
@@ -226,25 +239,44 @@
         if 0 <= moment - 3 < count:
             wide, close = finish(moment - 3, swaps[moment - 3])
             wides.append(wide)
-            closes.append(close)
+            closes.append([close])
         if 0 <= moment - 4 < count:
-            closes.extend(forward(moment - 4, wides[moment - 4]))
-    for copy in closes:
+            closes[moment - 4].extend(forward(moment - 4, wides[moment - 4]))
+        if moment >= count and len(earlies) < EARLY:
+            while sum(size for _, size in bounds[:arrived]) < (len(earlies) + 1) * unit:
+                for copy in closes[arrived]:
+                    copy.wait_recv()
+                arrived += 1
+            earlies.append(early_tile(len(earlies)))
+    for copy in sum(closes[arrived:], []):
         copy.wait_recv()
-    for copy in gathers + nears + sum(fars, []) + swaps + sum(wides, []) + closes:
+    sent = gathers + nears + sum(fars, []) + swaps + sum(wides, []) + sum(closes, [])
+    for copy in sent:
         copy.wait_send()
+    for copy in earlies:
+        copy.wait()
+
+
+def outer_tile(left_ref, right_ref, start, height, store):
+    rows, columns = right_ref.shape
+    width = min(256, columns)
+    left = left_ref[:, :, pl.ds(start, height)].reshape(rows, height)
+    for low in range(0, columns, width):
+        store(low, width, lax.dot_general(
+            left, right_ref[:, low:low + width],
+            (((0,), (0,)), ((), ())), preferred_element_type=jnp.float32,
+        ).astype(jnp.bfloat16))
 
 
 SLOTS = 4
 
 
-def gradient_kernel(height, left_ref, right_ref, out_hbm, tiles, sems):
-    rows, columns = right_ref.shape
-    count = out_hbm.shape[0] // height
-    width = min(256, columns)
+def gradient_kernel(height, left_ref, right_ref, early_hbm, out_hbm, tiles, held, sems, held_in, held_out):
+    ready = held.shape[0]
+    count = (out_hbm.shape[0] - ready) // height
 
     def copy_out(index, slot):
-        start = pl.multiple_of(index * height, height)
+        start = pl.multiple_of(ready + index * height, 128)
         return pltpu.make_async_copy(tiles.at[slot], out_hbm.at[pl.ds(start, height)], sems.at[slot])
 
     def tile(index, carry):
@@ -254,19 +286,25 @@
         def _():
             copy_out(index - SLOTS, slot).wait()
 
-        start = pl.multiple_of(index * height, height)
-        left = left_ref[:, :, pl.ds(start, height)].reshape(rows, height)
-        for low in range(0, columns, width):
-            tiles[slot, :, low:low + width] = lax.dot_general(
-                left, right_ref[:, low:low + width],
-                (((0,), (0,)), ((), ())), preferred_element_type=jnp.float32,
-            ).astype(tiles.dtype)
+        def store(low, width, value):
+            tiles[slot, :, low:low + width] = value
+
+        start = pl.multiple_of(ready + index * height, 128)
+        outer_tile(left_ref, right_ref, start, height, store)
         copy_out(index, slot).start()
         return carry
 
-    lax.fori_loop(0, count, tile, 0)
+    bring = pltpu.make_async_copy(early_hbm, held, held_in)
+    bring.start()
+    split = count // 2
+    lax.fori_loop(0, split, tile, 0)
+    bring.wait()
+    put = pltpu.make_async_copy(held, out_hbm.at[pl.ds(0, ready)], held_out)
+    put.start()
+    lax.fori_loop(split, count, tile, 0)
     for index in range(max(0, count - SLOTS), count):
         copy_out(index, index % SLOTS).wait()
+    put.wait()
 
 
 def local(sections, tensors, inputs, cotangent, plan, weights):
@@ -279,17 +317,19 @@
     unit = unit_of(hidden)
     bounds = chunk_bounds(hidden)
     count = len(bounds)
+    ready = EARLY * unit
     vmem = pl.BlockSpec(memory_space=pltpu.VMEM)
 
     dma = pltpu.SemaphoreType.DMA
-    left, right = pl.pallas_call(
+    left, right, early = pl.pallas_call(
         functools.partial(exchange_kernel, sections, tensors, bounds, unit),
         out_shape=(
             jax.ShapeDtypeStruct((tensors, block_rows, hidden), jnp.bfloat16),
             jax.ShapeDtypeStruct((row_count, columns), jnp.bfloat16),
+            jax.ShapeDtypeStruct((ready, columns), jnp.bfloat16),
         ),
         in_specs=[pl.BlockSpec(memory_space=pltpu.SMEM), vmem, vmem, pl.BlockSpec(memory_space=pl.ANY)],
-        out_specs=(vmem, vmem),
+        out_specs=(vmem, vmem, pl.BlockSpec(memory_space=pl.ANY)),
         scratch_shapes=[
             pltpu.VMEM((hidden, columns), jnp.bfloat16),
             pltpu.VMEM((2, shard_rows, columns), jnp.float32),
@@ -302,7 +342,8 @@
             pltpu.VMEM((block_rows, hidden), jnp.float32),
             pltpu.VMEM((block_rows, hidden), jnp.bfloat16),
             pltpu.VMEM((block_rows, hidden), jnp.bfloat16),
-            dma((count,)),
+            pltpu.VMEM((EARLY, unit, columns), jnp.bfloat16),
+            dma((hidden // unit,)),
             dma((sections,)),
             dma((sections,)),
             dma((count,)),
@@ -315,6 +356,7 @@
             dma((count, groups)),
             dma((count, groups)),
             dma((count, groups)),
+            dma((EARLY,)),
         ],
         compiler_params=pltpu.CompilerParams(
             collective_id=0, has_side_effects=True, vmem_limit_bytes=56 * 1024 * 1024
@@ -326,20 +368,26 @@
         ),
     )(plan, inputs, cotangent, weights[0])
 
-    height = next(h for h in (256, 128) if hidden % h == 0)
+    height = next(h for h in (256, 128) if (hidden - ready) % h == 0)
     grads = pl.pallas_call(
         functools.partial(gradient_kernel, height),
         out_shape=jax.ShapeDtypeStruct((hidden, columns), jnp.bfloat16),
-        in_specs=[vmem, vmem],
+        in_specs=[vmem, vmem, pl.BlockSpec(memory_space=pl.ANY)],
         out_specs=pl.BlockSpec(memory_space=pl.ANY),
-        scratch_shapes=[pltpu.VMEM((SLOTS, height, columns), jnp.bfloat16), dma((SLOTS,))],
+        scratch_shapes=[
+            pltpu.VMEM((SLOTS, height, columns), jnp.bfloat16),
+            pltpu.VMEM((ready, columns), jnp.bfloat16),
+            dma((SLOTS,)),
+            dma,
+            dma,
+        ],
         compiler_params=pltpu.CompilerParams(vmem_limit_bytes=60 * 1024 * 1024),
         cost_estimate=pl.CostEstimate(
             flops=2 * row_count * hidden * columns,
             bytes_accessed=2 * hidden * columns,
             transcendentals=0,
         ),
-    )(left, right)
+    )(left, right, early)
     return grads.reshape(1, hidden, columns)
 
 

time: 53.8 us -> 57.7 us (1.072)
  Pallas kernels: 53.5 us -> 57 us
    pallas_call x1, Pallas kernels: 39.3 us -> 42.9 us  [local(): pl.pallas_call(functools.partial(exchange_kernel, sections, tensors, boun...]
where the time goes in v4:
time: 57.7 us; the launch traced here: 57 us
  Pallas kernels  57 us (99%)
    pallas_call x1, Pallas kernels, local(): pl.pallas_call(functools.partial(exchange_kernel, sections, tensors, boun...  42.9 us
    pallas_call x1, Pallas kernels, local(): pl.pallas_call(functools.partial(gradient_kernel, height), out_shape=jax....  14 us

profile of v4, /device:TPU:0, one launch (start us, length us, event | category | flops | bytes accessed | tf_op | source)
XLA Modules:
  0.0 57.0 jit_solution(13138508268279527987)
XLA Ops:
  0.0 42.9 %shard_map.46 = (bf16[4,16,6656]{2,1,0:T(8,128)(2,1)}, bf16[64,2048]{1,0:T(8,128)(2,1)}, bf16[1536,2048]{1,0:T(8,128)(2,1)}) custom-call(s32[4]{0:T(128)} %plan_ref.1, bf16[4,2,2048]{2,1,0:T(2,128)(2,1)} %inputs_ref.1, bf16[4,2,2048]{2,1,0:T(2,128)(2,1)} %cotangent_ref.1, bf16[6656,2048]{1,0:T(8,128)(2,1)} %bitcast.2), custom_call_target="tpu_custom_call" | custom-call | flops 1744830464 | bytes 27262976 | tf_op jit(solution)/shard_map/pallas_call | solution.py:324
  42.9 14.0 %shard_map.47 = bf16[6656,2048]{1,0:T(8,128)(2,1)} custom-call(bf16[4,16,6656]{2,1,0:T(8,128)(2,1)} %get-tuple-element.8.left_ref, bf16[64,2048]{1,0:T(8,128)(2,1)} %get-tuple-element.9.right_ref, bf16[1536,2048]{1,0:T(8,128)(2,1)} %get-tuple-element.10.early_hbm), custom_call_target="tpu_custom_call" | custom-call | flops 1744830464 | bytes 27262976 | tf_op jit(solution)/shard_map/pallas_call | solution.py:372

commit v5 on v2

--- a/solution.py
+++ b/solution.py
@@ -8,7 +8,7 @@
 from jax.sharding import PartitionSpec as P
 
 MESH = pl.DeviceIdType.MESH
-CHUNKS = 5
+SLOTS = 3
 
 
 def unit_of(hidden):
@@ -16,11 +16,8 @@
 
 
 def chunk_bounds(hidden):
-    unit = unit_of(hidden)
-    units = hidden // unit
-    count = min(CHUNKS, units)
-    edges = [-(-units * c // count) for c in range(count + 1)]
-    return [(low * unit, (high - low) * unit) for low, high in zip(edges, edges[1:])]
+    size = 1664 if hidden % 1664 == 0 else unit_of(hidden)
+    return [(low, size) for low in range(0, hidden, size)]
 
 
 def exchange_kernel(
@@ -100,17 +97,12 @@
         low, size = bounds[c]
         loads[c].wait()
 
-        def tile(index, carry):
-            start = pl.multiple_of(low + index * unit, 128)
-            product = lax.dot_general(
-                right_ref[...], weight[pl.ds(start, unit), :],
-                (((1,), (1,)), ((), ())), preferred_element_type=jnp.float32,
-            ).astype(jnp.bfloat16)
-            for t in range(tensors):
-                part[t % 2, t // 2, :, pl.ds(start, unit)] = product[t * block_rows:(t + 1) * block_rows]
-            return carry
-
-        lax.fori_loop(0, size // unit, tile, 0)
+        product = lax.dot_general(
+            weight[pl.ds(low, size), :], right_ref[...],
+            (((1,), (1,)), ((), ())), preferred_element_type=jnp.float32,
+        ).T.astype(jnp.bfloat16)
+        for t in range(tensors):
+            part[t % 2, t // 2, :, pl.ds(low, size)] = product[t * block_rows:(t + 1) * block_rows]
         lanes = pl.ds(low, size)
         copy = pltpu.make_async_remote_copy(
             src_ref=part.at[1 - parity, :, :, lanes],
@@ -235,17 +227,27 @@
         copy.wait_send()
 
 
-SLOTS = 4
-
-
 def gradient_kernel(height, left_ref, right_ref, out_hbm, tiles, sems):
     rows, columns = right_ref.shape
-    count = out_hbm.shape[0] // height
+    hidden = out_hbm.shape[0]
+    count = hidden // height
+    rest = hidden - count * height
     width = min(256, columns)
 
-    def copy_out(index, slot):
-        start = pl.multiple_of(index * height, height)
-        return pltpu.make_async_copy(tiles.at[slot], out_hbm.at[pl.ds(start, height)], sems.at[slot])
+    def copy_out(index, slot, size=height):
+        start = pl.multiple_of(index * height, 128)
+        return pltpu.make_async_copy(
+            tiles.at[slot, pl.ds(0, size)], out_hbm.at[pl.ds(start, size)], sems.at[slot]
+        )
+
+    def fill(index, slot, size):
+        start = pl.multiple_of(index * height, 128)
+        left = left_ref[:, :, pl.ds(start, size)].reshape(rows, size)
+        for low in range(0, columns, width):
+            tiles[slot, pl.ds(0, size), low:low + width] = lax.dot_general(
+                left, right_ref[:, low:low + width],
+                (((0,), (0,)), ((), ())), preferred_element_type=jnp.float32,
+            ).astype(tiles.dtype)
 
     def tile(index, carry):
         slot = lax.rem(index, SLOTS)
@@ -254,19 +256,22 @@
         def _():
             copy_out(index - SLOTS, slot).wait()
 
-        start = pl.multiple_of(index * height, height)
-        left = left_ref[:, :, pl.ds(start, height)].reshape(rows, height)
-        for low in range(0, columns, width):
-            tiles[slot, :, low:low + width] = lax.dot_general(
-                left, right_ref[:, low:low + width],
-                (((0,), (0,)), ((), ())), preferred_element_type=jnp.float32,
-            ).astype(tiles.dtype)
+        fill(index, slot, height)
         copy_out(index, slot).start()
         return carry
 
     lax.fori_loop(0, count, tile, 0)
-    for index in range(max(0, count - SLOTS), count):
+    first = max(0, count - SLOTS)
+    if rest:
+        if count >= SLOTS:
+            copy_out(first, first % SLOTS).wait()
+            first += 1
+        fill(count, count % SLOTS, rest)
+        copy_out(count, count % SLOTS, rest).start()
+    for index in range(first, count):
         copy_out(index, index % SLOTS).wait()
+    if rest:
+        copy_out(count, count % SLOTS, rest).wait()
 
 
 def local(sections, tensors, inputs, cotangent, plan, weights):
@@ -326,7 +331,7 @@
         ),
     )(plan, inputs, cotangent, weights[0])
 
-    height = next(h for h in (256, 128) if hidden % h == 0)
+    height = 2 * unit
     grads = pl.pallas_call(
         functools.partial(gradient_kernel, height),
         out_shape=jax.ShapeDtypeStruct((hidden, columns), jnp.bfloat16),

time: 53.8 us -> 54.3 us (level)
  Pallas kernels: 53.5 us -> 54.1 us
    pallas_call x1, Pallas kernels: 39.3 us -> 42.6 us  [local(): pl.pallas_call(functools.partial(exchange_kernel, sections, tensors, boun...]
    pallas_call x1, Pallas kernels: 14.1 us -> 11.5 us  [local(): pl.pallas_call(functools.partial(gradient_kernel, height), out_shape=jax....]
where the time goes in v5:
time: 54.3 us; the launch traced here: 54.1 us
  Pallas kernels  54.1 us (100%)
    pallas_call x1, Pallas kernels, local(): pl.pallas_call(functools.partial(exchange_kernel, sections, tensors, boun...  42.6 us
    pallas_call x1, Pallas kernels, local(): pl.pallas_call(functools.partial(gradient_kernel, height), out_shape=jax....  11.5 us

profile of v5, /device:TPU:0, one launch (start us, length us, event | category | flops | bytes accessed | tf_op | source)
XLA Modules:
  0.0 54.1 jit_solution(15486186722130633914)
XLA Ops:
  0.0 42.6 %shard_map.46 = (bf16[4,16,6656]{2,1,0:T(8,128)(2,1)}, bf16[64,2048]{1,0:T(8,128)(2,1)}) custom-call(s32[4]{0:T(128)} %plan_ref.1, bf16[4,2,2048]{2,1,0:T(2,128)(2,1)} %inputs_ref.1, bf16[4,2,2048]{2,1,0:T(2,128)(2,1)} %cotangent_ref.1, bf16[6656,2048]{1,0:T(8,128)(2,1)} %bitcast.2), custom_call_target="tpu_custom_call" | custom-call | flops 1744830464 | bytes 27262976 | tf_op jit(solution)/shard_map/pallas_call | solution.py:290
  42.6 11.5 %shard_map.47 = bf16[6656,2048]{1,0:T(8,128)(2,1)} custom-call(bf16[4,16,6656]{2,1,0:T(8,128)(2,1)} %get-tuple-element.7.left_ref, bf16[64,2048]{1,0:T(8,128)(2,1)} %get-tuple-element.8.right_ref), custom_call_target="tpu_custom_call" | custom-call | flops 1744830464 | bytes 27262976 | tf_op jit(solution)/shard_map/pallas_call | solution.py:335

commit v6 on v5

--- a/solution.py
+++ b/solution.py
@@ -8,6 +8,7 @@
 from jax.sharding import PartitionSpec as P
 
 MESH = pl.DeviceIdType.MESH
+CHUNKS = 5
 SLOTS = 3
 
 
@@ -16,8 +17,11 @@
 
 
 def chunk_bounds(hidden):
-    size = 1664 if hidden % 1664 == 0 else unit_of(hidden)
-    return [(low, size) for low in range(0, hidden, size)]
+    unit = unit_of(hidden)
+    units = hidden // unit
+    count = min(CHUNKS, units)
+    edges = [-(-units * c // count) for c in range(count + 1)]
+    return [(low * unit, (high - low) * unit) for low, high in zip(edges, edges[1:])]
 
 
 def exchange_kernel(
@@ -97,12 +101,17 @@
         low, size = bounds[c]
         loads[c].wait()
 
-        product = lax.dot_general(
-            weight[pl.ds(low, size), :], right_ref[...],
-            (((1,), (1,)), ((), ())), preferred_element_type=jnp.float32,
-        ).T.astype(jnp.bfloat16)
-        for t in range(tensors):
-            part[t % 2, t // 2, :, pl.ds(low, size)] = product[t * block_rows:(t + 1) * block_rows]
+        def tile(index, carry):
+            start = pl.multiple_of(low + index * unit, 128)
+            product = lax.dot_general(
+                weight[pl.ds(start, unit), :], right_ref[...],
+                (((1,), (1,)), ((), ())), preferred_element_type=jnp.float32,
+            ).T.astype(jnp.bfloat16)
+            for t in range(tensors):
+                part[t % 2, t // 2, :, pl.ds(start, unit)] = product[t * block_rows:(t + 1) * block_rows]
+            return carry
+
+        lax.fori_loop(0, size // unit, tile, 0)
         lanes = pl.ds(low, size)
         copy = pltpu.make_async_remote_copy(
             src_ref=part.at[1 - parity, :, :, lanes],

time: 54.3 us -> 51.2 us (0.943)
  Pallas kernels: 54.1 us -> 50.8 us
    pallas_call x1, Pallas kernels: 42.6 us -> 39.2 us  [local(): pl.pallas_call(functools.partial(exchange_kernel, sections, tensors, boun...]
where the time goes in v6:
time: 51.2 us; the launch traced here: 50.8 us
  Pallas kernels  50.8 us (99%)
    pallas_call x1, Pallas kernels, local(): pl.pallas_call(functools.partial(exchange_kernel, sections, tensors, boun...  39.2 us
    pallas_call x1, Pallas kernels, local(): pl.pallas_call(functools.partial(gradient_kernel, height), out_shape=jax....  11.5 us

profile of v6, /device:TPU:0, one launch (start us, length us, event | category | flops | bytes accessed | tf_op | source)
XLA Modules:
  0.0 50.8 jit_solution(9882569384784652687)
XLA Ops:
  0.0 39.2 %shard_map.46 = (bf16[4,16,6656]{2,1,0:T(8,128)(2,1)}, bf16[64,2048]{1,0:T(8,128)(2,1)}) custom-call(s32[4]{0:T(128)} %plan_ref.1, bf16[4,2,2048]{2,1,0:T(2,128)(2,1)} %inputs_ref.1, bf16[4,2,2048]{2,1,0:T(2,128)(2,1)} %cotangent_ref.1, bf16[6656,2048]{1,0:T(8,128)(2,1)} %bitcast.2), custom_call_target="tpu_custom_call" | custom-call | flops 1744830464 | bytes 27262976 | tf_op jit(solution)/shard_map/pallas_call | solution.py:299
  39.3 11.5 %shard_map.47 = bf16[6656,2048]{1,0:T(8,128)(2,1)} custom-call(bf16[4,16,6656]{2,1,0:T(8,128)(2,1)} %get-tuple-element.7.left_ref, bf16[64,2048]{1,0:T(8,128)(2,1)} %get-tuple-element.8.right_ref), custom_call_target="tpu_custom_call" | custom-call | flops 1744830464 | bytes 27262976 | tf_op jit(solution)/shard_map/pallas_call | solution.py:344
